TPU v7x, 32 devices: a whole 2x2x4 slice. The times are simulated.
32 devices in a mesh: dp: 8 (over z, x), tensor: 4 (over y, core).
Axes of the slice: x: 2, y: 2, z: 4, core: 2. Of those that a mesh axis runs over, the one named last changes fastest.
Arguments:
- hidden: float32 [8192, 640], P('dp'), may hold values from -6 to 6
- seq_lengths: int32 [8, 4], P('dp'), may hold values from 0 to 1024, as said below
- input_scale: float32 [640], replicated, may hold values from 0.25 to 1.75
- w_query: float32 [640, 1024], P(None, 'tensor'), may hold values from -0.25 to 0.25
- w_key: float32 [640, 256], replicated, may hold values from -0.25 to 0.25
- w_value: float32 [640, 256], replicated, may hold values from -0.25 to 0.25
- query_scale: float32 [256], replicated, may hold values from 0.25 to 1.75
- key_scale: float32 [256], replicated, may hold values from 0.25 to 1.75
- w_out: float32 [1024, 640], P('tensor'), may hold values from -0.1875 to 0.1875
- post_attn_scale: float32 [640], replicated, may hold values from 0.25 to 1.75
- pre_ffn_scale: float32 [640], replicated, may hold values from 0.25 to 1.75
- w_gate: float32 [640, 2048], P(None, 'tensor'), may hold values from -0.25 to 0.25
- w_up: float32 [640, 2048], P(None, 'tensor'), may hold values from -0.25 to 0.25
- w_down: float32 [2048, 640], P('tensor'), may hold values from -0.125 to 0.125
- post_ffn_scale: float32 [640], replicated, may hold values from 0.25 to 1.75
- out_cotangent: float32 [8192, 640], P('dp'), may hold values from -6 to 6
Outputs:
- output: float32 [8192, 640], P('dp')
- hidden_grad: float32 [8192, 640], P('dp')
- input_scale_grad: float32 [640], replicated
- w_query_grad: float32 [640, 1024], P(None, 'tensor')
- w_key_grad: float32 [640, 256], replicated
- w_value_grad: float32 [640, 256], replicated
- query_scale_grad: float32 [256], replicated
- key_scale_grad: float32 [256], replicated
- w_out_grad: float32 [1024, 640], P('tensor')
- post_attn_scale_grad: float32 [640], replicated
- pre_ffn_scale_grad: float32 [640], replicated
- w_gate_grad: float32 [640, 2048], P(None, 'tensor')
- w_up_grad: float32 [640, 2048], P(None, 'tensor')
- w_down_grad: float32 [2048, 640], P('tensor')
- post_ffn_scale_grad: float32 [640], replicated
Inputs may be any that keep to these rules, and one draw needn't show every extreme that they name: `seq_lengths`: row d lists the lengths of the sequences held by index d of dp, in slot order, zeros for unused sequence slots; a row sums to at most 1024. In every draw exactly one row is a single sequence of 1024 tokens followed by zeros; every other row sums to between 128 and 896.
All inputs are finite; a program needn't handle non-finite values.
Results may differ from a plain program's by a relative error of at most 0.0003.
Values sent between devices are 32-bit elements; how exact they have to be, the bound alone decides.
A program may use at most 128 MiB of HBM per device.

v0:
```python
from functools import partial

import jax
import jax.numpy as jnp
from jax import lax
from jax.sharding import PartitionSpec as P

WINDOW = 512


epsilon = 1e-06
highest = lax.Precision.HIGHEST


def root_scale(values, gain):
    return values * lax.rsqrt(jnp.mean(values * values, axis=-1, keepdims=True) + epsilon) * gain


def rotate(values, cosine, sine):
    half_dim = values.shape[-1] // 2
    first_half = values[..., :half_dim]
    second_half = values[..., half_dim:]
    return jnp.concatenate(
        [first_half * cosine - second_half * sine, second_half * cosine + first_half * sine],
        axis=-1,
    )


def layout(lengths, row_count):
    bounds = jnp.concatenate([jnp.zeros((1,), jnp.int32), jnp.cumsum(lengths)])
    slot_index = jnp.arange(row_count, dtype=jnp.int32)
    segment = jnp.sum((slot_index[:, None] >= bounds[None, 1:]).astype(jnp.int32), axis=1)
    starts = jnp.max(jnp.where(bounds[None, :] <= slot_index[:, None], bounds[None, :], 0), axis=1)
    return (segment, slot_index - starts, slot_index < bounds[-1], slot_index)


def tables(positions, head_dim):
    half_dim = head_dim // 2
    frequency = 10000.0 ** (-2.0 * jnp.arange(half_dim).astype(jnp.float32) / head_dim)
    angles = positions.astype(jnp.float32)[:, None] * frequency[None, :]
    return (jnp.cos(angles), jnp.sin(angles))


def project_rows(inputs, gain, query_w, key_w, value_w, query_gain, key_gain, cosine, sine):
    normed = root_scale(inputs, gain)
    row_count = inputs.shape[0]
    queries = jnp.dot(normed, query_w, precision=highest).reshape(row_count, -1, key_w.shape[1])
    key_rows = jnp.dot(normed, key_w, precision=highest)
    value_rows = jnp.dot(normed, value_w, precision=highest)
    queries = rotate(root_scale(queries, query_gain), cosine[:, None, :], sine[:, None, :])
    key_rows = rotate(root_scale(key_rows, key_gain), cosine, sine)
    return (queries, key_rows, value_rows)


def middle(residual, branch, branch_gain, next_gain):
    hid_rows = residual + root_scale(branch, branch_gain)
    return (hid_rows, root_scale(hid_rows, next_gain))


def feed(inputs, gate_w, up_w, down_w):
    gated = jax.nn.gelu(jnp.dot(inputs, gate_w, precision=highest), approximate=True) * jnp.dot(
        inputs, up_w, precision=highest
    )
    return jnp.dot(gated, down_w, precision=highest)


def finish(branch, gain, residual):
    return residual + root_scale(branch, gain)


def on_device(
    hidden,
    seq_lengths,
    input_scale,
    w_query,
    w_key,
    w_value,
    query_scale,
    key_scale,
    w_out,
    post_attn_scale,
    pre_ffn_scale,
    w_gate,
    w_up,
    w_down,
    post_ffn_scale,
    out_cotangent,
):
    row_count = hidden.shape[0]
    head_dim = w_key.shape[1]
    head_count = w_query.shape[1] // head_dim
    scale = head_dim ** (-0.5)
    segment, positions, live_mask, slot_index = layout(seq_lengths[0], row_count)
    cosine, sine = tables(positions, head_dim)
    live_rows = live_mask.astype(jnp.float32)[:, None]
    (queries, key_rows, value_rows), project_back = jax.vjp(
        partial(project_rows, cosine=cosine, sine=sine),
        hidden,
        input_scale,
        w_query,
        w_key,
        w_value,
        query_scale,
        key_scale,
    )
    block_rows = min(512, row_count)
    block_count = row_count // block_rows
    key_pad = jnp.concatenate([jnp.zeros((block_rows, head_dim), jnp.float32), key_rows], axis=0)
    value_pad = jnp.concatenate(
        [jnp.zeros((block_rows, head_dim), jnp.float32), value_rows], axis=0
    )
    segment_pad = jnp.concatenate([jnp.full((block_rows,), -1, jnp.int32), segment])
    slot_pad = jnp.concatenate([jnp.arange(-block_rows, 0, dtype=jnp.int32), slot_index])

    def block_inputs(block_index):
        first_row = block_index * block_rows
        query_block = lax.dynamic_slice_in_dim(queries, first_row, block_rows, 0)
        key_block = lax.dynamic_slice_in_dim(key_pad, first_row, 2 * block_rows, 0)
        value_block = lax.dynamic_slice_in_dim(value_pad, first_row, 2 * block_rows, 0)
        distance = (
            lax.dynamic_slice_in_dim(slot_index, first_row, block_rows, 0)[:, None]
            - lax.dynamic_slice_in_dim(slot_pad, first_row, 2 * block_rows, 0)[None, :]
        )
        same_segment = (
            lax.dynamic_slice_in_dim(segment, first_row, block_rows, 0)[:, None]
            == lax.dynamic_slice_in_dim(segment_pad, first_row, 2 * block_rows, 0)[None, :]
        )
        allowed = same_segment & (distance >= 0) & (distance < WINDOW)
        scores = jnp.einsum("ihd,jd->hij", query_block, key_block, precision=highest) * scale
        scores = jnp.where(allowed[None], scores, -1e30)
        return (query_block, key_block, value_block, allowed, scores)

    def attend_block(block_index):
        query_block, key_block, value_block, allowed, scores = block_inputs(block_index)
        row_max = jnp.max(scores, axis=-1, keepdims=True)
        weights = jnp.exp(scores - row_max)
        weight_sum = jnp.sum(weights, axis=-1, keepdims=True)
        mixed_block = jnp.einsum(
            "hij,jd->ihd", weights / weight_sum, value_block, precision=highest
        )
        return (mixed_block, (row_max + jnp.log(weight_sum))[..., 0])

    def forward_block(block_index):
        return attend_block(block_index)

    mixed_blocks, log_sums = lax.map(forward_block, jnp.arange(block_count))
    mixed = mixed_blocks.reshape(row_count, head_count * head_dim)
    attn_part = jnp.dot(mixed, w_out, precision=highest)
    attn_whole = lax.psum(attn_part, "tensor")
    (hid_rows, ffn_in), middle_back = jax.vjp(
        middle, hidden, attn_whole, post_attn_scale, pre_ffn_scale
    )
    mlp_part, feed_back = jax.vjp(feed, ffn_in, w_gate, w_up, w_down)
    mlp_whole = lax.psum(mlp_part, "tensor")
    result, finish_back = jax.vjp(finish, mlp_whole, post_ffn_scale, hid_rows)
    output = result * live_rows
    out_grad = out_cotangent * live_rows
    mlp_grad, post_ffn_grad, hid_direct = finish_back(out_grad)
    ffn_in_part, gate_grad, up_grad, down_grad = feed_back(mlp_grad)
    ffn_in_grad = lax.psum(ffn_in_part, "tensor")
    hidden_direct, attn_grad, post_attn_grad, pre_ffn_grad = middle_back((hid_direct, ffn_in_grad))
    mixed_grad = jnp.dot(attn_grad, w_out.T, precision=highest).reshape(
        row_count, head_count, head_dim
    )
    out_weight_grad = jnp.dot(mixed.T, attn_grad, precision=highest)
    row_dots = jnp.sum(mixed_grad * mixed_blocks.reshape(row_count, head_count, head_dim), axis=-1)

    def attend_back(running, block_index):
        key_acc, value_acc = running
        query_block, key_block, value_block, allowed, scores = block_inputs(block_index)
        first_row = block_index * block_rows
        grad_block = lax.dynamic_slice_in_dim(mixed_grad, first_row, block_rows, 0)
        dots_block = lax.dynamic_slice_in_dim(row_dots, first_row, block_rows, 0)
        weights = jnp.where(allowed[None], jnp.exp(scores - log_sums[block_index][:, :, None]), 0.0)
        value_part = jnp.einsum("hij,ihd->jd", weights, grad_block, precision=highest)
        spread = jnp.einsum("ihd,jd->hij", grad_block, value_block, precision=highest)
        score_grad = weights * (spread - dots_block.T[:, :, None])
        query_part = jnp.einsum("hij,jd->ihd", score_grad, key_block, precision=highest) * scale
        key_part = jnp.einsum("hij,ihd->jd", score_grad, query_block, precision=highest) * scale
        key_acc = lax.dynamic_update_slice_in_dim(
            key_acc,
            lax.dynamic_slice_in_dim(key_acc, first_row, 2 * block_rows, 0) + key_part,
            first_row,
            0,
        )
        value_acc = lax.dynamic_update_slice_in_dim(
            value_acc,
            lax.dynamic_slice_in_dim(value_acc, first_row, 2 * block_rows, 0) + value_part,
            first_row,
            0,
        )
        return ((key_acc, value_acc), query_part)

    def back_block(running, block_index):
        return attend_back(running, block_index)

    empty_pad = jnp.zeros((row_count + block_rows, head_dim), jnp.float32)
    (key_acc, value_acc), query_parts = lax.scan(
        back_block, (empty_pad, empty_pad), jnp.arange(block_count)
    )
    query_grad = query_parts.reshape(row_count, head_count, head_dim)
    (
        hidden_part,
        input_part,
        query_w_grad,
        key_w_grad,
        value_w_grad,
        query_gain_grad,
        key_gain_grad,
    ) = project_back((query_grad, key_acc[block_rows:], value_acc[block_rows:]))
    hidden_attn, input_grad = lax.psum((hidden_part, input_part), "tensor")
    hidden_grad = hidden_direct + hidden_attn
    (
        query_w_grad,
        out_weight_grad,
        gate_grad,
        up_grad,
        down_grad,
        input_grad,
        post_attn_grad,
        pre_ffn_grad,
        post_ffn_grad,
    ) = lax.psum(
        (
            query_w_grad,
            out_weight_grad,
            gate_grad,
            up_grad,
            down_grad,
            input_grad,
            post_attn_grad,
            pre_ffn_grad,
            post_ffn_grad,
        ),
        "dp",
    )
    key_w_grad, value_w_grad, query_gain_grad, key_gain_grad = lax.psum(
        (key_w_grad, value_w_grad, query_gain_grad, key_gain_grad), ("dp", "tensor")
    )
    return (
        output,
        hidden_grad,
        input_grad,
        query_w_grad,
        key_w_grad,
        value_w_grad,
        query_gain_grad,
        key_gain_grad,
        out_weight_grad,
        post_attn_grad,
        pre_ffn_grad,
        gate_grad,
        up_grad,
        down_grad,
        post_ffn_grad,
    )


def solution(mesh):
    placed = (
        P("dp", None),
        P("dp", None),
        P(),
        P(None, "tensor"),
        P(),
        P(),
        P(),
        P(),
        P("tensor", None),
        P(),
        P(),
        P(None, "tensor"),
        P(None, "tensor"),
        P("tensor", None),
        P(),
        P("dp", None),
    )
    return jax.shard_map(
        on_device,
        mesh=mesh,
        in_specs=placed,
        out_specs=(
            P("dp", None),
            P("dp", None),
            P(),
            P(None, "tensor"),
            P(),
            P(),
            P(),
            P(),
            P("tensor", None),
            P(),
            P(),
            P(None, "tensor"),
            P(None, "tensor"),
            P("tensor", None),
            P(),
        ),
        check_vma=False,
    )
```

profile of v0, /device:TPU:0, one launch (start us, length us, event | category | flops | bytes accessed | tf_op | source)
XLA Modules:
  0.0 843.5 jit_solution(12557632794079602929)
XLA Ops:
  11.1 4.9 fusion.136
  23.3 4.9 multiply_reduce_fusion.15
  40.6 44.3 %while.26 = (s32[]{:T(128)}, f32[2,512,1,256]{1,0,3,2:T(2,128)}, f32[2,1,512]{2,1,0:T(1,128)}, s32[2]{0:T(128)S(1)}, f32[1536,256]{1,0:T(8,128)}, /*index=5*/s32...) while((s32[]{:T(128)}, f32[2,512,1,256]{1,0,3,2:T(2,128)}, ...), condition=%wide.region_9.10_spmd, body=%wide.region_6.9_spmd.sunk | while | flops 3228040704 | bytes 18932016 | solution.py:146
  52.4 10.3 %dynamic_update_slice.26 = f32[2,512,1,256]{1,0,3,2:T(2,128)} dynamic-update-slice(f32[2,512,1,256]{1,0,3,2:T(2,128)} %get-tuple-element.486, f32[1,512,1,256]{1,0,3,2:T(1,128)S(1)} %copy.111, s32[]{:T(128)S(6)} %copy.125, s32[]{:T(128)} %constant.60.clone.1..sunk, s32[]{:T(128)} %constant.60.clone.1..sunk, s32[]{:T(128)} %constant.60.clone.1..sunk) | dynamic-update-slice | bytes 1048580 | tf_op jit(solution)/shard_map/while/body/jit(dynamic_update_index_in_dim)/dynamic_update_slice | solution.py:146
  74.5 10.3 %dynamic_update_slice.26 = f32[2,512,1,256]{1,0,3,2:T(2,128)} dynamic-update-slice(f32[2,512,1,256]{1,0,3,2:T(2,128)} %get-tuple-element.486, f32[1,512,1,256]{1,0,3,2:T(1,128)S(1)} %copy.111, s32[]{:T(128)S(6)} %copy.125, s32[]{:T(128)} %constant.60.clone.1..sunk, s32[]{:T(128)} %constant.60.clone.1..sunk, s32[]{:T(128)} %constant.60.clone.1..sunk) | dynamic-update-slice | bytes 1048580 | tf_op jit(solution)/shard_map/while/body/jit(dynamic_update_index_in_dim)/dynamic_update_slice | solution.py:146
  91.9 62.3 %all-reduce.18.cloned.1.call-done = f32[1024,640]{1,0:T(8,128)} async-done(((f32[1024,640]{1,0:T(8,128)}), f32[1024,640]{1,0:T(8,128)}) %all-reduce.18.cloned.1.call-update) | async-done | bytes 2621456 | tf_op jit(solution)/shard_map/psum | solution.py:149
  159.3 5.1 fusion.70
  164.5 5.1 fusion.69
  171.0 7.4 fusion.121
  180.3 58.3 %all-reduce.20.cloned.1.call-done = f32[1024,640]{1,0:T(8,128)} async-done(((f32[1024,640]{1,0:T(8,128)}), f32[1024,640]{1,0:T(8,128)}) %all-reduce.20.cloned.1.call-update) | async-done | bytes 2621456 | tf_op jit(solution)/shard_map/psum | solution.py:154
  241.1 4.9 multiply_reduce_fusion
  246.2 5.6 fusion.133
  251.8 5.8 fusion.124
  257.7 8.5 %convolution_add_fusion = f32[1024,640]{1,0:T(8,128)} fusion(f32[1024,640]{1,0:T(8,128)S(1)} %fusion.124, f32[640,512]{1,0:T(8,128)S(1)} %copy-done.61, f32[1024,512]{1,0:T(8,128)S(1)} %copy-done.29, f32[1024,512]{1,0:T(8,128)S(1)} %fusion.133, f32[1024,512]{1,0:T(8,128)S(1)} %copy-done.44), kind=kOutput, calls=%fused_computation.94 | convolution fusion | flops 4037672960 | bytes 12845056 | tf_op jit(solution)/shard_map/transpose(jvp())/dot_general | solution.py:61
  266.3 9.4 %fusion.67 = f32[640,512]{1,0:T(8,128)} fusion(f32[1024,640]{1,0:T(8,128)} %copy-done.6, f32[640]{0:T(1024)S(1)} %copy-done.77, f32[1024]{0:T(1024)S(1)} %fusion.117, f32[1024,512]{1,0:T(8,128)} %copy-done.46, f32[1024,512]{1,0:T(8,128)} %copy-done.28), kind=kOutput, calls=%fused_computation.95 | convolution fusion | flops 4032561152 | bytes 8133120 | tf_op jit(solution)/shard_map/transpose(jvp())/dot_general | solution.py:61
  275.8 7.2 fusion.68
  283.0 43.4 %all-reduce.22.cloned.1.call-done = f32[1024,640]{1,0:T(8,128)} async-done(((f32[1024,640]{1,0:T(8,128)}), f32[1024,640]{1,0:T(8,128)}) %all-reduce.22.cloned.1.call-update) | async-done | bytes 2621456 | tf_op jit(solution)/shard_map/psum | solution.py:160
  334.2 4.3 multiply_reduce_fusion.14
  342.3 68.0 %while.27 = (s32[]{:T(128)}, f32[1536,256]{0,1:T(8,128)}, f32[1536,256]{1,0:T(8,128)}, f32[2,512,1,256]{1,0,3,2:T(2,128)}, s32[2]{0:T(128)S(1)}, /*index=5*/s32[...) while((s32[]{:T(128)}, f32[1536,256]{0,1:T(8,128)}, ...), condition=%wide.region_21.22_spmd, body=%wide.region_20.21_spmd.sunk | while | flops 8060272640 | bytes 59294212 | solution.py:198
  366.0 10.3 %dynamic_update_slice.29 = f32[2,512,1,256]{1,0,3,2:T(2,128)} dynamic-update-slice(f32[2,512,1,256]{1,0,3,2:T(2,128)} %get-tuple-element.541, f32[1,512,1,256]{1,0,3,2:T(1,128)S(1)} %copy.116, s32[]{:T(128)S(6)} %copy.138, s32[]{:T(128)} %constant.60.clone.1..sunk.1, s32[]{:T(128)} %constant.60.clone.1..sunk.1, s32[]{:T(128)} %constant.60.clone.1..sunk.1) | dynamic-update-slice | bytes 1048580 | tf_op jit(solution)/shard_map/while/body/jit(dynamic_update_index_in_dim)/dynamic_update_slice | solution.py:146
  399.9 10.3 %dynamic_update_slice.29 = f32[2,512,1,256]{1,0,3,2:T(2,128)} dynamic-update-slice(f32[2,512,1,256]{1,0,3,2:T(2,128)} %get-tuple-element.541, f32[1,512,1,256]{1,0,3,2:T(1,128)S(1)} %copy.116, s32[]{:T(128)S(6)} %copy.138, s32[]{:T(128)} %constant.60.clone.1..sunk.1, s32[]{:T(128)} %constant.60.clone.1..sunk.1, s32[]{:T(128)} %constant.60.clone.1..sunk.1) | dynamic-update-slice | bytes 1048580 | tf_op jit(solution)/shard_map/while/body/jit(dynamic_update_index_in_dim)/dynamic_update_slice | solution.py:146
  421.4 5.2 fusion.130
  430.7 6.1 multiply_reduce_fusion.3
  440.6 10.8 %fusion.119 = f32[512,640]{1,0:T(8,128)} fusion(f32[1024,512]{1,0:T(8,128)} %copy-done.43, f32[1024,512]{1,0:T(8,128)S(1)} %copy-done.31, f32[1024,640]{1,0:T(8,128)} %all-reduce.20.cloned.1.call-done, f32[1024,640]{1,0:T(8,128)} %param.35, f32[1024]{0:T(1024)S(1)} %copy-done.93, f32[1024]{0:T(1024)S(1)} %copy-done.76, f32[640]{0:T(1024)S(1)} %copy-done.91, ...), kind=kOutput, calls=%fused_computation.188 | convolution fusion | flops 4035182592 | bytes 10762752 | tf_op jit(solution)/shard_map/transpose(jvp())/dot_general | solution.py:64
  451.4 6.6 fusion.82
  458.1 5.6 fusion.129
  463.9 7.3 fusion.126
  475.3 39.7 %all-reduce.7 = (f32[256]{0:T(256)}, f32[256]{0:T(256)}) all-reduce(f32[256]{0:T(256)S(1)} %get-tuple-element.219, f32[256]{0:T(256)S(1)} %get-tuple-element.217), channel_id=1, replica_groups=mesh['dp'=8,'tensor'=4] {'dp','tensor'}, use_global_device_ids=true, to_apply=%region_33.34 | all-reduce | flops 512 | bytes 4096 | tf_op jit(solution)/shard_map/psum | solution.py:237
  515.0 7.1 psum.130
  522.0 36.2 %all-reduce.9 = (f32[640]{0:T(1024)}, f32[640]{0:T(1024)}, f32[640]{0:T(1024)}, f32[640]{0:T(1024)}) all-reduce(f32[640]{0:T(1024)S(1)} %psum.130, f32[640]{0:T(1024)S(1)} %get-tuple-element.213, f32[640]{0:T(1024)S(1)} %get-tuple-element.211, f32[640]{0:T(1024)S(1)} %copy-done.94), channel_id=1, replica_groups=mesh['dp'=8,'tensor'=4] {'dp'}, use_global_device_ids=true, to_apply=%region_28.29 | all-reduce | flops 2560 | bytes 20480 | tf_op jit(solution)/shard_map/psum | solution.py:223
  562.5 75.1 %all-reduce.26.cloned.1.call-done = (f32[640,256]{1,0:T(8,128)}, f32[640,256]{1,0:T(8,128)}) async-done(((f32[640,256]{1,0:T(8,128)}, f32[640,256]{1,0:T(8,128)}), (f32[640,256]{1,0:T(8,128)}, f32[640,256]{1,0:T(8,128)})) %all-reduce.26.cloned.1.call-update) | async-done | bytes 1310736 | tf_op jit(solution)/shard_map/psum | solution.py:237
  637.6 189.8 %all-reduce.28.cloned.1.call-done = (f32[640,256]{1,0:T(8,128)}, f32[256,640]{1,0:T(8,128)}, f32[640,512]{1,0:T(8,128)}, f32[640,512]{1,0:T(8,128)}, f32[512,640]{1,0:T(8,128)}) async-done(((f32[640,256]{1,0:T(8,128)}, f32[256,640]{1,0:T(8,128)}, f32[640,512]{1,0:T(8,128)}, f32[640,512]{1,0:T(8,128)}, f32[512,640]{1,0:T(8,128)}), (f32[640,256]{1,0:T(8,128)}, f32[256,640]{1,0:T(8,128)}, ...) | async-done | bytes 5242896 | tf_op jit(solution)/shard_map/psum | solution.py:223
  (351 shorter events, 153.1 us)
Async XLA Ops:
  7.2 163.9 %copy-start = (f32[512,640]{1,0:T(8,128)S(1)}, f32[512,640]{1,0:T(8,128)}, u32[]{:S(2)}) copy-start(f32[512,640]{1,0:T(8,128)} %param.33) | copy-start | bytes 3932164
  7.2 147.0 %all-reduce.18.cloned.1.call-start = ((), (), s32[]{:S(2)}) async-start(), calls=%async_computation | async-start | bytes 5242880 | tf_op jit(solution)/shard_map/psum | solution.py:149
  7.3 21.2 %copy-start.95 = (f32[128]{0:T(128)}, f32[128]{0:T(128)S(1)}, u32[]{:S(2)}) copy-start(f32[128]{0:T(128)S(1)} %multiply_power_fusion) | copy-start | bytes 1540
  8.2 7.8 copy-start.97
  9.1 19.4 %copy-start.67 = (f32[1024]{0:T(1024)}, f32[1024]{0:T(1024)S(1)}, u32[]{:S(2)}) copy-start(f32[1024]{0:T(1024)S(1)} %subtract_convert_fusion) | copy-start | bytes 12292
  91.5 64.9 %copy-start.73 = (f32[640]{0:T(1024)S(1)}, f32[640]{0:T(1024)}, u32[]{:S(2)}) copy-start(f32[640]{0:T(1024)} %param.29) | copy-start | bytes 7684
  91.5 147.1 %all-reduce.20.cloned.1.call-start = ((), (), s32[]{:S(2)}) async-start(), calls=%async_computation.1 | async-start | bytes 5242880 | tf_op jit(solution)/shard_map/psum | solution.py:154
  156.8 177.4 %copy-start.65 = (f32[1024]{0:T(1024)}, f32[1024]{0:T(1024)S(1)}, u32[]{:S(2)}) copy-start(f32[1024]{0:T(1024)S(1)} %fusion.116) | copy-start | bytes 12292
  178.4 62.3 %copy-start.90 = (f32[640]{0:T(1024)S(1)}, f32[640]{0:T(1024)}, u32[]{:S(2)}) copy-start(f32[640]{0:T(1024)} %param.34) | copy-start | bytes 7684
  178.4 148.0 %all-reduce.22.cloned.1.call-start = ((), (), s32[]{:S(2)}) async-start(), calls=%async_computation.2 | async-start | bytes 5242880 | tf_op jit(solution)/shard_map/psum | solution.py:160
  180.3 149.7 %copy-start.75 = (f32[1024]{0:T(1024)}, f32[1024]{0:T(1024)S(1)}, u32[]{:S(2)}) copy-start(f32[1024]{0:T(1024)S(1)} %fusion.112) | copy-start | bytes 12292
  266.3 292.0 %all-reduce.24.cloned.1.call-start = ((), (), s32[]{:S(2)}) async-start(), calls=%async_computation.3 | async-start | bytes 5242880 | tf_op jit(solution)/shard_map/psum | solution.py:211
  266.3 9.4 %copy-start.8 = (f32[1024,640]{1,0:T(8,128)S(1)}, f32[1024,640]{1,0:T(8,128)}, u32[]{:S(2)}) copy-start(f32[1024,640]{1,0:T(8,128)} %copy-done.6) | copy-start | bytes 7864324
  266.3 9.4 %copy-start.30 = (f32[1024,512]{1,0:T(8,128)S(1)}, f32[1024,512]{1,0:T(8,128)}, u32[]{:S(2)}) copy-start(f32[1024,512]{1,0:T(8,128)} %copy-done.28) | copy-start | bytes 6291460
  266.3 9.4 %copy-start.45 = (f32[1024,512]{1,0:T(8,128)S(1)}, f32[1024,512]{1,0:T(8,128)}, u32[]{:S(2)}) copy-start(f32[1024,512]{1,0:T(8,128)} %copy-done.43) | copy-start | bytes 6291460
  266.3 9.4 %copy-start.47 = (f32[1024,512]{1,0:T(8,128)S(1)}, f32[1024,512]{1,0:T(8,128)}, u32[]{:S(2)}) copy-start(f32[1024,512]{1,0:T(8,128)} %copy-done.46) | copy-start | bytes 6291460
  364.9 11.5 %copy-start.17 = (f32[1024,1,256]{2,1,0:T(1,128)S(1)}, f32[1024,1,256]{2,1,0:T(1,128)}, u32[]{:S(2)}) copy-start(f32[1024,1,256]{2,1,0:T(1,128)} %copy-done.16) | copy-start | bytes 3145732 | tf_op jit(solution)/shard_map/while
  398.8 11.5 %copy-start.17 = (f32[1024,1,256]{2,1,0:T(1,128)S(1)}, f32[1024,1,256]{2,1,0:T(1,128)}, u32[]{:S(2)}) copy-start(f32[1024,1,256]{2,1,0:T(1,128)} %copy-done.16) | copy-start | bytes 3145732 | tf_op jit(solution)/shard_map/while
  410.3 7.1 copy-start.14
  417.3 13.4 %copy-start.35 = (f32[1024,1,128]{0,2,1:T(8,128)}, f32[1024,1,128]{0,2,1:T(8,128)S(1)}, u32[]{:S(2)}) copy-start(f32[1024,1,128]{0,2,1:T(8,128)S(1)} %get-tuple-element.294) | copy-start | bytes 1572868
  417.3 13.4 %copy-start.37 = (f32[1024,1,128]{0,2,1:T(8,128)}, f32[1024,1,128]{0,2,1:T(8,128)S(1)}, u32[]{:S(2)}) copy-start(f32[1024,1,128]{0,2,1:T(8,128)S(1)} %get-tuple-element.295) | copy-start | bytes 1572868
  439.0 198.6 %all-reduce.26.cloned.1.call-start = ((), (), s32[]{:S(2)}) async-start(), calls=%async_computation.4 | async-start | bytes 2621440 | tf_op jit(solution)/shard_map/psum | solution.py:237
  440.6 10.8 %copy-start.5 = (f32[1024,640]{1,0:T(8,128)S(1)}, f32[1024,640]{1,0:T(8,128)}, u32[]{:S(2)}) copy-start(f32[1024,640]{1,0:T(8,128)} %param.20) | copy-start | bytes 7864324
  451.4 6.7 copy-start.42
  463.7 7.4 copy-start.34
  463.8 7.4 copy-start.66
  463.8 7.4 copy-start.74
  463.8 363.7 %all-reduce.28.cloned.1.call-start = ((), (), s32[]{:S(2)}) async-start(), calls=%async_computation.5 | async-start | bytes 10485760 | tf_op jit(solution)/shard_map/psum | solution.py:223
  463.8 7.3 copy-start.11
  463.9 7.3 copy-start.13
  475.2 46.8 %copy-start.94 = (f32[640]{0:T(1024)S(1)}, f32[640]{0:T(1024)}, u32[]{:S(2)}) copy-start(f32[640]{0:T(1024)} %get-tuple-element.209) | copy-start | bytes 7684
  637.6 193.9 %copy-start.62 = (f32[640,256]{1,0:T(8,128)S(1)}, f32[640,256]{1,0:T(8,128)}, u32[]{:S(2)}) copy-start(f32[640,256]{1,0:T(8,128)} %get-tuple-element.585) | copy-start | bytes 1966084
  (79 other events, 285.1 us)
Sparse Core Ops, SparseCore 0:
  91.6 62.5 all-reduce.17
  178.5 59.9 all-reduce.19
  266.4 59.9 all-reduce.21
  439.1 60.6 all-reduce.23
  505.9 131.7 all-reduce.25
  643.0 184.4 all-reduce.27
where the time goes:
time: 852 us; the launch traced here: 844 us
  waiting for transfers between devices  429 us (50%)
  matrix products  165 us (19%)
  local copies, waits for them, and re-layouts  100 us (12%)
  blocking collectives  82.9 us (10%)
  other arithmetic  43.3 us (5%)
  between operations  15.5 us (2%)
    psum x1, waiting for transfers between devices, on_device(): lax.psum((query_w_grad, out_weight_grad, gate_grad, up_grad, down_grad, i...  190 us
    psum x1, waiting for transfers between devices, on_device(): lax.psum((key_w_grad, value_w_grad, query_gain_grad, key_gain_grad), ('dp...  75.1 us
    psum x1, waiting for transfers between devices, on_device(): attn_whole = lax.psum(attn_part, 'tensor')  62.3 us
    psum x1, waiting for transfers between devices, on_device(): mlp_whole = lax.psum(mlp_part, 'tensor')  58.3 us
    dynamic_update_slice x10, local copies, waits for them, and re-layouts, on_device(): mixed_blocks, log_sums = lax.map(forward_block, jnp.arange(block_count))  44.6 us
    psum x1, waiting for transfers between devices, on_device(): ffn_in_grad = lax.psum(ffn_in_part, 'tensor')  43.4 us
    psum x1, blocking collectives, on_device(): lax.psum((key_w_grad, value_w_grad, query_gain_grad, key_gain_grad), ('dp...  39.7 us
    psum x1, blocking collectives, on_device(): lax.psum((query_w_grad, out_weight_grad, gate_grad, up_grad, down_grad, i...  36.2 us
  transfers between devices with their start and end apart: 6, of which 5 were waited for; matrix products, arithmetic and copies ran while one was open for 7% of the time, Pallas kernels for 0%

commit v1 on v0

v1 whole, which is shorter than its diff:
```python
from functools import partial

import jax
import jax.numpy as jnp
from jax import lax
from jax.experimental import pallas as pl
from jax.experimental.pallas import tpu as pltpu
from jax.sharding import PartitionSpec as P

WINDOW = 512


epsilon = 1e-06
highest = lax.Precision.HIGH


def root_scale(values, gain):
    return values * lax.rsqrt(jnp.mean(values * values, axis=-1, keepdims=True) + epsilon) * gain


def rotate(values, cosine, sine):
    half_dim = values.shape[-1] // 2
    first_half = values[..., :half_dim]
    second_half = values[..., half_dim:]
    return jnp.concatenate(
        [first_half * cosine - second_half * sine, second_half * cosine + first_half * sine],
        axis=-1,
    )


def layout(lengths, row_count):
    count = lengths.shape[0]
    before = jnp.arange(count)[:, None] < jnp.arange(count + 1)[None, :]
    bounds = jnp.sum(jnp.where(before, lengths[:, None], 0), axis=0)
    slot_index = jnp.arange(row_count, dtype=jnp.int32)
    segment = jnp.sum((slot_index[:, None] >= bounds[None, 1:]).astype(jnp.int32), axis=1)
    starts = jnp.max(jnp.where(bounds[None, :] <= slot_index[:, None], bounds[None, :], 0), axis=1)
    return (segment, slot_index - starts, slot_index < bounds[-1], slot_index)


def tables(positions, head_dim):
    half_dim = head_dim // 2
    frequency = 10000.0 ** (-2.0 * jnp.arange(half_dim).astype(jnp.float32) / head_dim)
    angles = positions.astype(jnp.float32)[:, None] * frequency[None, :]
    return (jnp.cos(angles), jnp.sin(angles))


def middle(residual, branch, branch_gain, next_gain):
    hid_rows = residual + root_scale(branch, branch_gain)
    return (hid_rows, root_scale(hid_rows, next_gain))


def feed(inputs, gate_w, up_w, down_w):
    gated = jax.nn.gelu(jnp.dot(inputs, gate_w, precision=highest), approximate=True) * jnp.dot(
        inputs, up_w, precision=highest
    )
    return jnp.dot(gated, down_w, precision=highest)


def finish(branch, gain, residual):
    return residual + root_scale(branch, gain)


def share_kernel(chunks, x_ref, out_ref, near, total, far, sems):
    me = lax.axis_index("tensor")
    side = lax.rem(me, 2)
    near_dev = me + 1 - 2 * side
    far_dev = lax.rem(me + 2, 4)
    barrier = pltpu.get_barrier_semaphore()
    for partner in (near_dev, far_dev):
        pl.semaphore_signal(
            barrier, inc=1, device_id={"tensor": partner}, device_id_type=pl.DeviceIdType.MESH
        )
    pl.semaphore_wait(barrier, 2)
    half = x_ref.shape[0] // 2
    size = half // chunks

    def rows(first, c):
        return pl.ds(pl.multiple_of(first * half + c * size, 8), size)

    def send(stage, c, source, target, device):
        copy = pltpu.make_async_remote_copy(
            src_ref=source,
            dst_ref=target,
            send_sem=sems.at[stage, 0, c],
            recv_sem=sems.at[stage, 1, c],
            device_id={"tensor": device},
            device_id_type=pl.DeviceIdType.MESH,
        )
        copy.start()
        return copy

    first = [
        send(0, c, x_ref.at[rows(1 - side, c)], near.at[pl.ds(c * size, size)], near_dev)
        for c in range(chunks)
    ]
    second = []
    for c in range(chunks):
        here = pl.ds(c * size, size)
        first[c].wait_recv()
        total[here] = x_ref[rows(side, c)] + near[here]
        second.append(send(1, c, total.at[here], far.at[here], far_dev))
    third = []
    for c in range(chunks):
        here = pl.ds(c * size, size)
        second[c].wait_recv()
        out_ref[rows(side, c)] = total[here] + far[here]
        third.append(send(2, c, out_ref.at[rows(side, c)], out_ref.at[rows(side, c)], near_dev))
    for c in range(chunks):
        third[c].wait_recv()
    for copy in first + second + third:
        copy.wait_send()


def share(x, collective_id, chunks):
    if lax.axis_size("tensor") != 4:
        return lax.psum(x, "tensor")
    row_count, width = x.shape
    half = (row_count // 2, width)
    return pl.pallas_call(
        partial(share_kernel, chunks),
        out_shape=jax.ShapeDtypeStruct(x.shape, jnp.float32),
        in_specs=[pl.BlockSpec(memory_space=pltpu.VMEM)],
        out_specs=pl.BlockSpec(memory_space=pltpu.VMEM),
        scratch_shapes=[
            pltpu.VMEM(half, jnp.float32),
            pltpu.VMEM(half, jnp.float32),
            pltpu.VMEM(half, jnp.float32),
            pltpu.SemaphoreType.DMA((3, 2, chunks)),
        ],
        compiler_params=pltpu.CompilerParams(
            collective_id=collective_id, has_side_effects=True, vmem_limit_bytes=32 * 2**20
        ),
        cost_estimate=pl.CostEstimate(
            flops=x.size * 2, bytes_accessed=x.size * 8, transcendentals=0
        ),
    )(x)


def heads(projected, query_gain, key_gain, cosine, sine):
    head_dim = key_gain.shape[0]
    value_cols = projected.shape[1] - head_dim
    key_cols = value_cols - head_dim
    row_count = projected.shape[0]
    queries = projected[:, :key_cols].reshape(row_count, -1, head_dim)
    queries = rotate(root_scale(queries, query_gain), cosine[:, None, :], sine[:, None, :])
    key_rows = rotate(root_scale(projected[:, key_cols:value_cols], key_gain), cosine, sine)
    return (queries, key_rows, projected[:, value_cols:])


def dot(a, b, dims):
    return lax.dot_general(
        a, b, (dims, ((), ())), precision=highest, preferred_element_type=jnp.float32
    )


rows_rows = ((0,), (0,))
plain = ((1,), (0,))
cols_cols = ((1,), (1,))


def on_device(
    hidden,
    seq_lengths,
    input_scale,
    w_query,
    w_key,
    w_value,
    query_scale,
    key_scale,
    w_out,
    post_attn_scale,
    pre_ffn_scale,
    w_gate,
    w_up,
    w_down,
    post_ffn_scale,
    out_cotangent,
):
    row_count, width = hidden.shape
    head_dim = w_key.shape[1]
    head_count = w_query.shape[1] // head_dim
    scale = head_dim ** (-0.5)
    segment, positions, live_mask, slot_index = layout(seq_lengths[0], row_count)
    cosine, sine = tables(positions, head_dim)
    live_rows = live_mask.astype(jnp.float32)[:, None]
    normed, input_back = jax.vjp(root_scale, hidden, input_scale)
    w_all = jnp.concatenate([w_query, w_key, w_value], axis=1)
    projected = dot(normed, w_all, plain)
    (queries, key_rows, value_rows), heads_back = jax.vjp(
        partial(heads, cosine=cosine, sine=sine), projected, query_scale, key_scale
    )
    block_rows = min(WINDOW, row_count)
    block_count = row_count // block_rows
    kept = []
    mixed_heads = [[] for _ in range(head_count)]
    for b in range(block_count):
        q_rows = slice(b * block_rows, (b + 1) * block_rows)
        k_rows = slice(max(b - 1, 0) * block_rows, (b + 1) * block_rows)
        distance = slot_index[q_rows, None] - slot_index[None, k_rows]
        allowed = (
            (segment[q_rows, None] == segment[None, k_rows])
            & (distance >= 0)
            & (distance < WINDOW)
        )
        for h in range(head_count):
            scores = dot(queries[q_rows, h], key_rows[k_rows], cols_cols) * scale
            scores = jnp.where(allowed, scores, -1e30)
            weights = jnp.exp(scores - jnp.max(scores, axis=-1, keepdims=True))
            weights = weights / jnp.sum(weights, axis=-1, keepdims=True)
            kept.append((q_rows, k_rows, h, weights))
            mixed_heads[h].append(dot(weights, value_rows[k_rows], plain))
    mixed = jnp.concatenate([jnp.concatenate(m, axis=0) for m in mixed_heads], axis=1)
    attn_whole = share(dot(mixed, w_out, plain), 0, 4)
    (hid_rows, ffn_in), middle_back = jax.vjp(
        middle, hidden, attn_whole, post_attn_scale, pre_ffn_scale
    )
    gate = dot(ffn_in, w_gate, plain)
    up = dot(ffn_in, w_up, plain)
    gated, gated_back = jax.vjp(lambda g, u: jax.nn.gelu(g, approximate=True) * u, gate, up)
    mlp_whole = share(dot(gated, w_down, plain), 0, 4)
    result, finish_back = jax.vjp(finish, mlp_whole, post_ffn_scale, hid_rows)
    output = result * live_rows
    out_grad = out_cotangent * live_rows
    mlp_grad, post_ffn_grad, hid_direct = finish_back(out_grad)
    gate_back, up_back = gated_back(dot(mlp_grad, w_down, cols_cols))
    down_grad = dot(gated, mlp_grad, rows_rows)
    gate_grad = dot(ffn_in, gate_back, rows_rows)
    up_grad = dot(ffn_in, up_back, rows_rows)
    ffn_in_part = dot(gate_back, w_gate, cols_cols) + dot(up_back, w_up, cols_cols)
    ffn_in_part, gate_grad, up_grad, down_grad = lax.optimization_barrier(
        (ffn_in_part, gate_grad, up_grad, down_grad)
    )
    early = lax.psum((gate_grad, up_grad, down_grad), "dp")
    ffn_in_grad = share(ffn_in_part, 0, 4)
    hidden_direct, attn_grad, post_attn_grad, pre_ffn_grad = middle_back((hid_direct, ffn_in_grad))
    mixed_grad = dot(attn_grad, w_out, cols_cols)
    out_weight_grad = dot(mixed, attn_grad, rows_rows)
    query_parts = [[] for _ in range(head_count)]
    key_blocks = [0.0] * block_count
    value_blocks = [0.0] * block_count
    for q_rows, k_rows, h, weights in kept:
        cols = slice(h * head_dim, (h + 1) * head_dim)
        grad_block = mixed_grad[q_rows, cols]
        row_dots = jnp.sum(grad_block * mixed[q_rows, cols], axis=-1, keepdims=True)
        value_part = dot(weights, grad_block, rows_rows)
        spread = dot(grad_block, value_rows[k_rows], cols_cols)
        score_grad = weights * (spread - row_dots) * scale
        query_parts[h].append(dot(score_grad, key_rows[k_rows], plain))
        key_part = dot(score_grad, queries[q_rows, h], rows_rows)
        for i in range((k_rows.stop - k_rows.start) // block_rows):
            b = k_rows.start // block_rows + i
            part = slice(i * block_rows, (i + 1) * block_rows)
            key_blocks[b] = key_blocks[b] + key_part[part]
            value_blocks[b] = value_blocks[b] + value_part[part]
    query_grad = jnp.stack([jnp.concatenate(q, axis=0) for q in query_parts], axis=1)
    projected_grad, query_gain_grad, key_gain_grad = heads_back(
        (query_grad, jnp.concatenate(key_blocks, axis=0), jnp.concatenate(value_blocks, axis=0))
    )
    normed_part = dot(projected_grad, w_all, cols_cols)
    w_all_grad = dot(projected_grad, normed, rows_rows)
    query_cols = head_count * head_dim
    shared = share(jnp.concatenate([normed_part, w_all_grad[query_cols:]], axis=0), 1, 6)
    hidden_attn, input_grad = input_back(shared[:row_count])
    hidden_grad = hidden_direct + hidden_attn
    tensor_size = lax.axis_size("tensor")
    me = lax.axis_index("tensor")
    quarter = 2 * head_dim // tensor_size
    kv_quarter = lax.dynamic_slice_in_dim(shared, row_count + me * quarter, quarter, 0)
    fill = jnp.zeros((width - 2 * head_dim,), jnp.float32)
    gains = jnp.stack(
        [
            jnp.concatenate([query_gain_grad, key_gain_grad, fill]),
            input_grad,
            post_attn_grad,
            pre_ffn_grad,
            post_ffn_grad,
        ]
        + [jnp.zeros((width,), jnp.float32)] * 3
    )
    late = jnp.concatenate([w_all_grad[:query_cols], kv_quarter, gains], axis=0)
    late, early = lax.optimization_barrier((late, early))
    late, out_weight_grad = lax.psum((late, out_weight_grad), "dp")
    gate_grad, up_grad, down_grad = early
    piece = quarter + 8
    spread_rows = lax.dynamic_update_slice_in_dim(
        jnp.zeros((tensor_size * piece, width), jnp.float32),
        late[query_cols : query_cols + piece],
        me * piece,
        0,
    )
    gathered = share(spread_rows, 2, 2).reshape(tensor_size, piece, width)
    kv_grad = gathered[:, :quarter].reshape(2 * head_dim, width)
    head_gains = jnp.sum(gathered[:, quarter], axis=0)
    gains = late[query_cols + quarter :]
    return (
        output,
        hidden_grad,
        gains[1],
        late[:query_cols].T,
        kv_grad[:head_dim].T,
        kv_grad[head_dim:].T,
        head_gains[:head_dim],
        head_gains[head_dim : 2 * head_dim],
        out_weight_grad,
        gains[2],
        gains[3],
        gate_grad,
        up_grad,
        down_grad,
        gains[4],
    )


def solution(mesh):
    placed = (
        P("dp", None),
        P("dp", None),
        P(),
        P(None, "tensor"),
        P(),
        P(),
        P(),
        P(),
        P("tensor", None),
        P(),
        P(),
        P(None, "tensor"),
        P(None, "tensor"),
        P("tensor", None),
        P(),
        P("dp", None),
    )
    return jax.shard_map(
        on_device,
        mesh=mesh,
        in_specs=placed,
        out_specs=(
            P("dp", None),
            P("dp", None),
            P(),
            P(None, "tensor"),
            P(),
            P(),
            P(),
            P(),
            P("tensor", None),
            P(),
            P(),
            P(None, "tensor"),
            P(None, "tensor"),
            P("tensor", None),
            P(),
        ),
        check_vma=False,
    )
```

time: 852 us -> 447 us (0.52)
  waiting for transfers between devices: 429 us -> 105 us
  Pallas kernels: 0 us -> 173 us
  blocking collectives: 82.9 us -> 0 us
  matrix products: 165 us -> 87.9 us
  local copies, waits for them, and re-layouts: 100 us -> 31.5 us
  other arithmetic: 43.3 us -> 28.5 us
    psum x6 -> x2, waiting for transfers between devices: 429 us -> 105 us  [the longest x1 89.5 us: on_device(): late, out_weight_grad = lax.psum((late, out_weight_grad), 'dp')]
    pallas_call x0 -> x5, Pallas kernels: none -> 173 us  [share(): pl.pallas_call(partial(share_kernel, chunks), out_shape=jax.ShapeDtypeStr...]
    psum x3 -> x0, blocking collectives: 82.9 us -> none  [the longest x1 39.7 us: on_device(): lax.psum((key_w_grad, value_w_grad, query_gain_grad, key_gain_grad), ('dp...]
    dot_general x35 -> x27, matrix products: 165 us -> 87.9 us  [dot(): lax.dot_general(a, b, (dims, ((), ())), precision=highest, preferred_elem...]
    dynamic_update_slice x14 -> x1, local copies, waits for them, and re-layouts: 47.5 us -> 1.01 us  [on_device(): lax.dynamic_update_slice_in_dim(jnp.zeros((tensor_size * piece, width), j...]
    dynamic_slice x32 -> x1, local copies, waits for them, and re-layouts: 15.3 us -> 1.73 us  [on_device(): lax.dynamic_slice_in_dim(shared, row_count + me * quarter, quarter, 0)]
    unnamed x195 -> x113, local copies, waits for them, and re-layouts: 18.7 us -> 20.6 us
  transfers between devices with their start and end apart: 6 -> 2, of which waited for: 5 -> 2; matrix products, arithmetic and copies ran while one was open for 7% -> 11% of each run, Pallas kernels for 0% -> 19%
where the time goes in v1:
time: 447 us; the launch traced here: 441 us
  Pallas kernels  173 us (39%)
  waiting for transfers between devices  105 us (23%)
  matrix products  87.9 us (20%)
  local copies, waits for them, and re-layouts  31.5 us (7%)
  other arithmetic  28.5 us (6%)
  between operations  15.6 us (3%)
    pallas_call x5, Pallas kernels, share(): pl.pallas_call(partial(share_kernel, chunks), out_shape=jax.ShapeDtypeStr...  173 us
    psum x1, waiting for transfers between devices, on_device(): late, out_weight_grad = lax.psum((late, out_weight_grad), 'dp')  89.5 us
    dot_general x27, matrix products, dot(): lax.dot_general(a, b, (dims, ((), ())), precision=highest, preferred_elem...  87.9 us
    unnamed x113, local copies, waits for them, and re-layouts  20.6 us
    psum x1, waiting for transfers between devices, on_device(): early = lax.psum((gate_grad, up_grad, down_grad), 'dp')  15.3 us
  transfers between devices with their start and end apart: 2, of which 2 were waited for; matrix products, arithmetic and copies ran while one was open for 11% of the time, Pallas kernels for 19%

profile of v1, /device:TPU:0, one launch (start us, length us, event | category | flops | bytes accessed | tf_op | source)
XLA Modules:
  0.0 441.1 jit_solution(12271911693431529355)
XLA Ops:
  8.9 2.0 multiply_reduce_fusion.11
  12.7 4.3 fusion.5
  17.6 2.1 fusion.78
  19.7 2.4 fusion.74
  29.5 35.1 %shard_map.271 = f32[1024,640]{1,0:T(8,128)S(1)} custom-call(f32[1024,640]{1,0:T(8,128)S(1)} %fusion.56.x_ref), custom_call_target="tpu_custom_call" | custom-call | flops 1310720 | bytes 5242880 | tf_op jit(solution)/shard_map/pallas_call | solution.py:120
  66.9 2.7 fusion.24
  69.6 14.9 %fusion.23 = f32[1024,512]{1,0:T(8,128)S(1)} fusion(f32[640,512]{1,0:T(8,128)S(1)} %copy-done.18, f32[1024,640]{1,0:T(8,128)S(1)} %get-tuple-element.88, f32[640]{0:T(1024)S(1)} %copy-done.46, f32[1024]{0:T(1024)S(1)} %fusion.105), kind=kOutput, calls=%fused_computation.53 | convolution fusion | flops 2014576640 | bytes 6035968 | tf_op jit(solution)/shard_map/dot_general | solution.py:152
  84.4 3.2 fusion.123.x_ref
  87.7 34.2 %shard_map.272 = f32[1024,640]{1,0:T(8,128)S(1)} custom-call(f32[1024,640]{1,0:T(8,128)S(1)} %fusion.123.x_ref), custom_call_target="tpu_custom_call" | custom-call | flops 1310720 | bytes 5242880 | tf_op jit(solution)/shard_map/pallas_call | solution.py:120
  123.7 2.5 multiply_reduce_fusion
  126.2 5.0 %fusion.121 = f32[512,640]{1,0:T(8,128)} fusion(f32[1024,512]{1,0:T(8,128)S(1)} %fusion.23, f32[1024,512]{1,0:T(8,128)S(1)} %fusion.24, f32[1024,640]{1,0:T(8,128)S(1)} %shard_map.272, f32[1024,640]{1,0:T(8,128)S(1)} %copy-done.14, f32[1024]{0:T(1024)S(1)} %multiply_multiply_fusion.15, f32[1024]{0:T(1024)S(1)} %fusion.100, f32[640]{0:T(1024)S(1)} %copy-done.51, ...), kind=kOutput, calls=%fused_computation.213 | convolution fusion | flops 2021916672 | bytes 10762752 | tf_op jit(solution)/shard_map/dot_general | solution.py:152
  131.2 4.1 fusion.14
  135.3 3.7 fusion.22
  139.0 4.6 %fusion.138 = f32[1024,640]{1,0:T(8,128)} fusion(f32[1024,512]{1,0:T(8,128)S(1)} %get-tuple-element.110, f32[640,512]{1,0:T(8,128)S(1)} %copy-done.16), kind=kOutput, calls=%fused_computation.222 | convolution fusion | flops 2013265920 | bytes 6029312 | tf_op jit(solution)/shard_map/dot_general | solution.py:152
  143.6 4.0 fusion.21
  147.6 6.4 %convolution_add_fusion.x_ref = f32[1024,640]{1,0:T(8,128)S(1)} fusion(f32[1024,640]{1,0:T(8,128)} %fusion.138, f32[640,512]{1,0:T(8,128)} %param.28, f32[1024,512]{1,0:T(8,128)} %copy-done.35, f32[1024,512]{1,0:T(8,128)} %copy-done.13), kind=kOutput, calls=%fused_computation.50 | convolution fusion | flops 2018639872 | bytes 10747904 | tf_op jit(solution)/shard_map/dot_general | solution.py:152
  154.0 34.2 %shard_map.273 = f32[1024,640]{1,0:T(8,128)S(1)} custom-call(f32[1024,640]{1,0:T(8,128)S(1)} %convolution_add_fusion.x_ref), custom_call_target="tpu_custom_call" | custom-call | flops 1310720 | bytes 5242880 | tf_op jit(solution)/shard_map/pallas_call | solution.py:120
  190.9 1.9 multiply_reduce_fusion.2
  204.3 2.4 fusion.80
  207.1 2.3 fusion.76
  212.8 4.1 fusion.3
  218.2 10.2 %fusion.41 = f32[1024,640]{1,0:T(8,128)S(1)} fusion(f32[640,768]{1,0:T(8,128)} %copy-done.30, f32[512,256]{0,1:T(8,128)S(1)} %slice.188, f32[512,256]{0,1:T(8,128)} %copy-done.52, f32[1024,256]{0,1:T(8,128)} %copy-done.41, f32[1024,256]{0,1:T(8,128)} %copy-done.40), kind=kOutput, calls=%fused_computation.76 | convolution fusion | flops 3024617472 | bytes 7733248 | tf_op jit(solution)/shard_map/dot_general | solution.py:152
  228.7 48.3 %shard_map.274 = f32[1536,640]{1,0:T(8,128)S(1)} custom-call(f32[1536,640]{1,0:T(8,128)S(1)} %pad_maximum_fusion.x_ref), custom_call_target="tpu_custom_call" | custom-call | flops 1966080 | bytes 7864320 | tf_op jit(solution)/shard_map/pallas_call | solution.py:120
  277.1 1.9 copy-done.4
  281.4 3.8 concatenate.43
  285.2 4.9 %fusion.55 = f32[256,640]{1,0:T(8,128)} fusion(f32[512,256]{1,0:T(8,128)} %copy-done.23, f32[512,256]{1,0:T(8,128)} %copy-done.21, f32[1024,640]{1,0:T(8,128)S(1)} %copy-done.3, f32[1024,640]{1,0:T(8,128)} %copy-done.12, f32[1024]{0:T(1024)S(1)} %multiply_multiply_fusion.13, f32[640]{0:T(1024)S(1)} %copy-done.47, f32[1024]{0:T(1024)S(1)} %fusion.104), kind=kOutput, calls=%fused_computation.109 | convolution fusion | flops 1010171904 | bytes 6957568 | tf_op jit(solution)/shard_map/dot_general | solution.py:152
  290.2 15.3 %all-reduce.14.cloned.1.call-done = (f32[640,512]{1,0:T(8,128)}, f32[640,512]{1,0:T(8,128)}, f32[512,640]{1,0:T(8,128)}) async-done(((f32[640,512]{1,0:T(8,128)}, f32[640,512]{1,0:T(8,128)}, f32[512,640]{1,0:T(8,128)}), (f32[640,512]{1,0:T(8,128)}, f32[640,512]{1,0:T(8,128)}, f32[512,640]{1,0:T(8,128)})) %all-reduce.14.cloned.1.call-update) | async-done | bytes 3932176 | tf_op jit(solution)/shard_map/psum | solution.py:234
  305.5 5.4 %fusion.2 = f32[1024,640]{1,0:T(8,128)} fusion(f32[1024,640]{1,0:T(8,128)} %copy-done.12, f32[1024,640]{1,0:T(8,128)} %param.16, f32[1536,640]{1,0:T(8,128)} %copy-done.4, f32[1024]{0:T(1024)S(1)} %multiply_multiply_fusion.10, f32[640]{0:T(1024)S(1)} %copy-done.48, f32[1024]{0:T(1024)S(1)} %fusion.101), kind=kLoop, calls=%fused_computation.11 | loop fusion | flops 3932160 | bytes 10496512 | tf_op jit(solution)/shard_map/add | solution.py:265
  311.0 89.5 %all-reduce.12.cloned.1.call-done = (f32[392,640]{1,0:T(8,128)}, f32[256,640]{1,0:T(8,128)}) async-done(((f32[392,640]{1,0:T(8,128)}, f32[256,640]{1,0:T(8,128)}), (f32[392,640]{1,0:T(8,128)}, f32[256,640]{1,0:T(8,128)})) %all-reduce.12.cloned.1.call-update) | async-done | bytes 1658896 | tf_op jit(solution)/shard_map/psum | solution.py:283
  401.6 21.0 %shard_map.275 = f32[544,640]{1,0:T(8,128)S(1)} custom-call(f32[544,640]{1,0:T(8,128)S(1)} %slice_dynamic-update-slice_fusion.x_ref), custom_call_target="tpu_custom_call" | custom-call | flops 696320 | bytes 2785280 | tf_op jit(solution)/shard_map/pallas_call | solution.py:120
  427.1 2.0 copy.77
  429.1 2.6 copy.78
  (195 shorter events, 44.5 us)
Async XLA Ops:
  7.2 77.3 %copy-start = (f32[512,640]{1,0:T(8,128)S(1)}, f32[512,640]{1,0:T(8,128)}, u32[]{:S(2)}) copy-start(f32[512,640]{1,0:T(8,128)} %param.29) | copy-start | bytes 3932164
  7.2 3.8 copy-start.43
  7.2 3.9 copy-start.44
  7.2 298.3 %all-reduce.14.cloned.1.call-start = ((), (), s32[]{:S(2)}) async-start(), calls=%async_computation.1 | async-start | bytes 7864320 | tf_op jit(solution)/shard_map/psum | solution.py:234
  12.7 4.4 copy-start.30
  12.7 4.6 %copy-start.49 = (f32[256]{0:T(256)S(1)}, f32[256]{0:T(256)}, u32[]{:S(2)}) copy-start(f32[256]{0:T(256)} %param.23) | copy-start | bytes 3076
  12.7 4.6 %copy-start.50 = (f32[256]{0:T(256)S(1)}, f32[256]{0:T(256)}, u32[]{:S(2)}) copy-start(f32[256]{0:T(256)} %param.22) | copy-start | bytes 3076
  17.1 9.7 %copy-start.10 = (f32[1024,768]{0,1:T(8,128)}, f32[1024,768]{0,1:T(8,128)S(1)}, u32[]{:S(2)}) copy-start(f32[1024,768]{0,1:T(8,128)S(1)} %fusion.5) | copy-start | bytes 9437188
  19.7 4.7 %copy-start.19 = (f32[1024,128]{0,1:T(8,128)}, f32[1024,128]{0,1:T(8,128)S(1)}, u32[]{:S(2)}) copy-start(f32[1024,128]{0,1:T(8,128)S(1)} %get-tuple-element.101) | copy-start | bytes 1572868
  22.1 2.4 copy-start.25
  24.4 3.6 copy-start.21
  28.1 36.5 %copy-start.23 = (f32[512,256]{1,0:T(8,128)}, f32[512,256]{1,0:T(8,128)S(1)}, u32[]{:S(2)}) copy-start(f32[512,256]{1,0:T(8,128)S(1)} %fusion.49) | copy-start | bytes 1572868
  66.1 77.5 %copy-start.5 = (f32[1024,640]{1,0:T(8,128)}, f32[1024,640]{1,0:T(8,128)S(1)}, u32[]{:S(2)}) copy-start(f32[1024,640]{1,0:T(8,128)S(1)} %get-tuple-element.88) | copy-start | bytes 7864324
  66.9 2.7 copy-start.18
  69.6 74.1 %copy-start.13 = (f32[1024,512]{1,0:T(8,128)}, f32[1024,512]{1,0:T(8,128)S(1)}, u32[]{:S(2)}) copy-start(f32[1024,512]{1,0:T(8,128)S(1)} %fusion.24) | copy-start | bytes 6291460
  135.3 8.3 %copy-start.35 = (f32[1024,512]{1,0:T(8,128)}, f32[1024,512]{1,0:T(8,128)S(1)}, u32[]{:S(2)}) copy-start(f32[1024,512]{1,0:T(8,128)S(1)} %get-tuple-element.111) | copy-start | bytes 6291460
  154.0 246.5 %all-reduce.12.cloned.1.call-start = ((), (), s32[]{:S(2)}) async-start(), calls=%async_computation | async-start | bytes 3317760 | tf_op jit(solution)/shard_map/psum | solution.py:283
  154.0 34.2 %copy-start.6 = (f32[1024,640]{1,0:T(8,128)S(1)}, f32[1024,640]{1,0:T(8,128)}, u32[]{:S(2)}) copy-start(f32[1024,640]{1,0:T(8,128)} %copy-done.5) | copy-start | bytes 7864324
  188.3 2.6 copy-start.15
  192.8 5.3 %copy-start.12 = (f32[1024,640]{1,0:T(8,128)}, f32[1024,640]{1,0:T(8,128)S(1)}, u32[]{:S(2)}) copy-start(f32[1024,640]{1,0:T(8,128)S(1)} %get-tuple-element.86) | copy-start | bytes 7864324
  192.9 3.1 copy-start.11
  192.9 3.8 copy-start.34
  210.3 6.6 %copy-start.41 = (f32[1024,256]{0,1:T(8,128)}, f32[1024,256]{0,1:T(8,128)S(1)}, u32[]{:S(2)}) copy-start(f32[1024,256]{0,1:T(8,128)S(1)} %fusion.43) | copy-start | bytes 3145732
  210.3 2.4 copy-start.8
  212.8 4.1 copy-start.52
  218.2 10.2 %slice-start = ((f32[768,640]{1,0:T(8,128)}), f32[512,640]{1,0:T(8,128)S(1)}, s32[]{:S(2)}) async-start(f32[768,640]{1,0:T(8,128)} %copy-done.17), calls=%async_computation.2 | async-start | bytes 2621440 | tf_op jit(solution)/shard_map/slice | solution.py:263
  228.7 50.2 %copy-start.9 = (f32[1024,640]{1,0:T(8,128)S(1)}, f32[1024,640]{1,0:T(8,128)}, u32[]{:S(2)}) copy-start(f32[1024,640]{1,0:T(8,128)} %param.16) | copy-start | bytes 7864324
  279.0 2.5 slice-start.1
  401.6 21.1 %copy-start.42 = (f32[392,640]{1,0:T(8,128)S(1)}, f32[392,640]{1,0:T(8,128)}, u32[]{:S(2)}) copy-start(f32[392,640]{1,0:T(8,128)} %get-tuple-element.81) | copy-start | bytes 3010564
  426.1 5.7 %copy-start.37 = (f32[640,512]{1,0:T(8,128)S(1)}, f32[640,512]{1,0:T(8,128)}, u32[]{:S(2)}) copy-start(f32[640,512]{1,0:T(8,128)} %get-tuple-element.126) | copy-start | bytes 3932164
  429.1 3.7 copy-start.36
  429.1 4.7 %copy-start.1 = (f32[512,640]{1,0:T(8,128)S(1)}, f32[512,640]{1,0:T(8,128)}, u32[]{:S(2)}) copy-start(f32[512,640]{1,0:T(8,128)} %param.29) | copy-start | bytes 3932164
  (26 other events, 40.4 us)
Sparse Core Ops, SparseCore 0:
  154.1 151.3 all-reduce.13
  309.7 90.7 all-reduce.11

commit v2 on v1

--- a/solution.py
+++ b/solution.py
@@ -128,6 +128,156 @@
             pltpu.VMEM(half, jnp.float32),
             pltpu.SemaphoreType.DMA((3, 2, chunks)),
         ],
+        compiler_params=pltpu.CompilerParams(
+            collective_id=collective_id, has_side_effects=True, vmem_limit_bytes=32 * 2**20
+        ),
+        cost_estimate=pl.CostEstimate(
+            flops=x.size * 2, bytes_accessed=x.size * 8, transcendentals=0
+        ),
+    )(x)
+
+
+def gather_kernel(x_ref, out_ref, sems):
+    me = lax.axis_index("tensor")
+    side = lax.rem(me, 2)
+    near_dev = me + 1 - 2 * side
+    far_dev = lax.rem(me + 2, 4)
+    barrier = pltpu.get_barrier_semaphore()
+    for partner in (near_dev, far_dev):
+        pl.semaphore_signal(
+            barrier, inc=1, device_id={"tensor": partner}, device_id_type=pl.DeviceIdType.MESH
+        )
+    pl.semaphore_wait(barrier, 2)
+
+    def send(stage, source, slot, device):
+        copy = pltpu.make_async_remote_copy(
+            src_ref=source,
+            dst_ref=out_ref.at[slot],
+            send_sem=sems.at[stage, 0],
+            recv_sem=sems.at[stage, 1],
+            device_id={"tensor": device},
+            device_id_type=pl.DeviceIdType.MESH,
+        )
+        copy.start()
+        return copy
+
+    across = send(0, x_ref, me, far_dev)
+    beside = send(1, x_ref, me, near_dev)
+    out_ref[me] = x_ref[...]
+    across.wait_recv()
+    onward = send(2, out_ref.at[far_dev], far_dev, near_dev)
+    beside.wait_recv()
+    onward.wait_recv()
+    for copy in (across, beside, onward):
+        copy.wait_send()
+
+
+def gather(x, collective_id):
+    if lax.axis_size("tensor") != 4:
+        return lax.all_gather(x, "tensor")
+    return pl.pallas_call(
+        gather_kernel,
+        out_shape=jax.ShapeDtypeStruct((4, *x.shape), jnp.float32),
+        in_specs=[pl.BlockSpec(memory_space=pltpu.VMEM)],
+        out_specs=pl.BlockSpec(memory_space=pltpu.VMEM),
+        scratch_shapes=[pltpu.SemaphoreType.DMA((3, 2))],
+        compiler_params=pltpu.CompilerParams(
+            collective_id=collective_id, has_side_effects=True, vmem_limit_bytes=32 * 2**20
+        ),
+        cost_estimate=pl.CostEstimate(flops=0, bytes_accessed=x.size * 20, transcendentals=0),
+    )(x)
+
+
+def total_kernel(parts, x_ref, out_ref, total, landed, sems):
+    me = lax.axis_index("dp")
+    sides = [lax.rem(me // 2**bit, 2) for bit in range(3)]
+    partners = [me + (1 - 2 * sides[bit]) * 2**bit for bit in range(3)]
+    barrier = pltpu.get_barrier_semaphore()
+    for partner in partners:
+        pl.semaphore_signal(
+            barrier, inc=1, device_id={"dp": partner}, device_id_type=pl.DeviceIdType.MESH
+        )
+    pl.semaphore_wait(barrier, 3)
+
+    def span(first, size):
+        return pl.ds(pl.multiple_of(first, 8), size)
+
+    def send(stage, p, source, target, bit):
+        copy = pltpu.make_async_remote_copy(
+            src_ref=source,
+            dst_ref=target,
+            send_sem=sems.at[stage, 0, p],
+            recv_sem=sems.at[stage, 1, p],
+            device_id={"dp": partners[bit]},
+            device_id_type=pl.DeviceIdType.MESH,
+        )
+        copy.start()
+        copies.append(copy)
+        return copy
+
+    copies = []
+    pending = [None] * len(parts)
+    bases = [first for first, _, _ in parts]
+    slots = [first for first, _, _ in parts]
+
+    def halve(stage, p):
+        first, size, order = parts[p]
+        half = size // 2 ** (stage + 1)
+        bit = order[stage]
+        source = x_ref if stage == 0 else total
+        give = bases[p] + (1 - sides[bit]) * half
+        bases[p] = bases[p] + sides[bit] * half
+        pending[p] = send(
+            stage, p, source.at[span(give, half)], landed.at[pl.ds(slots[p], half)], bit
+        )
+
+    def double(stage, p):
+        size = parts[p][1] // 2 ** (stage + 1)
+        rows = out_ref.at[span(bases[p], size)]
+        bit = parts[p][2][stage]
+        pending[p] = send(5 - stage, p, rows, rows, bit)
+        bases[p] = bases[p] - sides[bit] * size
+
+    for p in range(len(parts)):
+        halve(0, p)
+    for stage in range(3):
+        for p in range(len(parts)):
+            half = parts[p][1] // 2 ** (stage + 1)
+            pending[p].wait_recv()
+            keep = span(bases[p], half)
+            source = x_ref if stage == 0 else total
+            target = out_ref if stage == 2 else total
+            target[keep] = source[keep] + landed[pl.ds(slots[p], half)]
+            slots[p] = slots[p] + half
+            if stage < 2:
+                halve(stage + 1, p)
+            else:
+                double(2, p)
+    for stage in (1, 0):
+        for p in range(len(parts)):
+            pending[p].wait_recv()
+            double(stage, p)
+    for p in range(len(parts)):
+        pending[p].wait_recv()
+    for copy in copies:
+        copy.wait_send()
+
+
+def total_rows(x, collective_id):
+    if lax.axis_size("dp") != 8:
+        return lax.psum(x, "dp")
+    row_count, width = x.shape
+    units = -(-row_count // 64)
+    x = jnp.pad(x, ((0, units * 64 - row_count), (0, 0)))
+    cut = (units + 1) // 2 * 64
+    parts = ((0, cut, (0, 1, 2)), (cut, x.shape[0] - cut, (1, 2, 0)))
+    whole = pltpu.VMEM(x.shape, jnp.float32)
+    return pl.pallas_call(
+        partial(total_kernel, parts),
+        out_shape=jax.ShapeDtypeStruct(x.shape, jnp.float32),
+        in_specs=[pl.BlockSpec(memory_space=pltpu.VMEM)],
+        out_specs=pl.BlockSpec(memory_space=pltpu.VMEM),
+        scratch_shapes=[whole, whole, pltpu.SemaphoreType.DMA((6, 2, len(parts)))],
         compiler_params=pltpu.CompilerParams(
             collective_id=collective_id, has_side_effects=True, vmem_limit_bytes=32 * 2**20
         ),
@@ -278,21 +428,16 @@
         ]
         + [jnp.zeros((width,), jnp.float32)] * 3
     )
-    late = jnp.concatenate([w_all_grad[:query_cols], kv_quarter, gains], axis=0)
-    late, early = lax.optimization_barrier((late, early))
-    late, out_weight_grad = lax.psum((late, out_weight_grad), "dp")
+    late = total_rows(
+        jnp.concatenate([w_all_grad[:query_cols], out_weight_grad, kv_quarter, gains], axis=0), 3
+    )
+    kv_first = query_cols + out_weight_grad.shape[0]
+    out_weight_grad = late[query_cols:kv_first]
     gate_grad, up_grad, down_grad = early
-    piece = quarter + 8
-    spread_rows = lax.dynamic_update_slice_in_dim(
-        jnp.zeros((tensor_size * piece, width), jnp.float32),
-        late[query_cols : query_cols + piece],
-        me * piece,
-        0,
-    )
-    gathered = share(spread_rows, 2, 2).reshape(tensor_size, piece, width)
+    gathered = gather(late[kv_first : kv_first + quarter + 8], 2)
     kv_grad = gathered[:, :quarter].reshape(2 * head_dim, width)
     head_gains = jnp.sum(gathered[:, quarter], axis=0)
-    gains = late[query_cols + quarter :]
+    gains = late[kv_first + quarter :]
     return (
         output,
         hidden_grad,

time: 447 us -> 401 us (0.90)
  waiting for transfers between devices: 105 us -> 0.02 us
  Pallas kernels: 173 us -> 228 us
    psum x1 -> x0, waiting for transfers between devices: 89.5 us -> none  [on_device(): late, out_weight_grad = lax.psum((late, out_weight_grad), 'dp')]
    pallas_call x0 -> x2, Pallas kernels: none -> 76.3 us  [the longest x1 64.9 us: total_rows(): pl.pallas_call(partial(total_kernel, parts), out_shape=jax.ShapeDtypeStru...]
    pallas_call x5 -> x4, Pallas kernels: 173 us -> 152 us  [share(): pl.pallas_call(partial(share_kernel, chunks), out_shape=jax.ShapeDtypeStr...]
    psum x1, waiting for transfers between devices: 15.3 us -> 0.01 us  [on_device(): early = lax.psum((gate_grad, up_grad, down_grad), 'dp')]
    unnamed x113 -> x120, local copies, waits for them, and re-layouts: 20.6 us -> 18.4 us
  transfers between devices with their start and end apart: 2 -> 1, of which waited for: 2 -> 0; matrix products, arithmetic and copies ran while one was open for 11% -> 15% of each run, Pallas kernels for 19% -> 40%
where the time goes in v2:
time: 401 us; the launch traced here: 394 us
  Pallas kernels  228 us (57%)
  matrix products  87.7 us (22%)
  local copies, waits for them, and re-layouts  34 us (8%)
  other arithmetic  28.8 us (7%)
  between operations  15.6 us (4%)
    pallas_call x4, Pallas kernels, share(): pl.pallas_call(partial(share_kernel, chunks), out_shape=jax.ShapeDtypeStr...  152 us
    dot_general x27, matrix products, dot(): lax.dot_general(a, b, (dims, ((), ())), precision=highest, preferred_elem...  87.7 us
    pallas_call x1, Pallas kernels, total_rows(): pl.pallas_call(partial(total_kernel, parts), out_shape=jax.ShapeDtypeStru...  64.9 us
    unnamed x120, local copies, waits for them, and re-layouts  18.4 us
    pallas_call x1, Pallas kernels, gather(): pl.pallas_call(gather_kernel, out_shape=jax.ShapeDtypeStruct((4, *x.shape...  11.4 us
  transfers between devices with their start and end apart: 1, of which 0 were waited for; matrix products, arithmetic and copies ran while one was open for 15% of the time, Pallas kernels for 40%

profile of v2, /device:TPU:0, one launch (start us, length us, event | category | flops | bytes accessed | tf_op | source)
XLA Modules:
  0.0 394.3 jit_solution(12718065095023232117)
XLA Ops:
  9.7 2.0 multiply_reduce_fusion.11
  13.5 4.3 %fusion.5 = f32[1024,768]{0,1:T(8,128)S(1)} fusion(f32[640,768]{1,0:T(8,128)S(1)} %constant_dynamic-update-slice_fusion, f32[1024,640]{1,0:T(8,128)S(1)} %copy-done.7, f32[640]{0:T(1024)S(1)} %copy-done.50, f32[1024]{0:T(1024)S(1)} %fusion.101), kind=kOutput, calls=%fused_computation.29 | convolution fusion | flops 3021209600 | bytes 7739904 | tf_op jit(solution)/shard_map/dot_general | solution.py:302
  18.4 2.1 fusion.74
  20.5 2.4 fusion.78
  30.2 35.1 %shard_map.271 = f32[1024,640]{1,0:T(8,128)S(1)} custom-call(f32[1024,640]{1,0:T(8,128)S(1)} %fusion.56.x_ref), custom_call_target="tpu_custom_call" | custom-call | flops 1310720 | bytes 5242880 | tf_op jit(solution)/shard_map/pallas_call | solution.py:120
  67.5 2.7 fusion.24
  70.2 14.8 %fusion.23 = f32[1024,512]{1,0:T(8,128)S(1)} fusion(f32[640,512]{1,0:T(8,128)S(1)} %copy-done.18, f32[1024,640]{1,0:T(8,128)S(1)} %get-tuple-element.78, f32[640]{0:T(1024)S(1)} %copy-done.48, f32[1024]{0:T(1024)S(1)} %fusion.105), kind=kOutput, calls=%fused_computation.53 | convolution fusion | flops 2014576640 | bytes 6035968 | tf_op jit(solution)/shard_map/dot_general | solution.py:302
  85.1 3.2 fusion.123.x_ref
  88.3 34.2 %shard_map.272 = f32[1024,640]{1,0:T(8,128)S(1)} custom-call(f32[1024,640]{1,0:T(8,128)S(1)} %fusion.123.x_ref), custom_call_target="tpu_custom_call" | custom-call | flops 1310720 | bytes 5242880 | tf_op jit(solution)/shard_map/pallas_call | solution.py:120
  124.2 2.5 multiply_reduce_fusion
  126.7 5.0 %fusion.121 = f32[512,640]{1,0:T(8,128)} fusion(f32[1024,512]{1,0:T(8,128)S(1)} %fusion.23, f32[1024,512]{1,0:T(8,128)S(1)} %fusion.24, f32[1024,640]{1,0:T(8,128)S(1)} %shard_map.272, f32[1024,640]{1,0:T(8,128)S(1)} %copy-done.14, f32[1024]{0:T(1024)S(1)} %multiply_multiply_fusion.15, f32[1024]{0:T(1024)S(1)} %fusion.100, f32[640]{0:T(1024)S(1)} %copy-done.55, ...), kind=kOutput, calls=%fused_computation.212 | convolution fusion | flops 2021916672 | bytes 10762752 | tf_op jit(solution)/shard_map/dot_general | solution.py:302
  131.7 4.1 %fusion.14 = (f32[1024,512]{1,0:T(8,128)S(1)}, f32[1024,512]{1,0:T(8,128)S(1)}) fusion(f32[1024,512]{1,0:T(8,128)S(1)} %fusion.24, f32[1024,512]{1,0:T(8,128)S(1)} %fusion.23, f32[512,640]{1,0:T(8,128)S(1)} %copy-done, f32[1024,640]{1,0:T(8,128)S(1)} %shard_map.272, f32[1024,640]{1,0:T(8,128)S(1)} %copy-done.14, f32[1024]{0:T(1024)S(1)} %multiply_multiply_fusion.15, ...), kind=kOutput, calls=%fused_computation.38 | convolution fusion | flops 2027683840 | bytes 14957056 | tf_op jit(solution)/shard_map/dot_general | solution.py:302
  135.8 3.7 fusion.22
  139.5 4.6 %fusion.139 = f32[1024,640]{1,0:T(8,128)} fusion(f32[1024,512]{1,0:T(8,128)S(1)} %get-tuple-element.102, f32[640,512]{1,0:T(8,128)S(1)} %copy-done.16), kind=kOutput, calls=%fused_computation.222 | convolution fusion | flops 2013265920 | bytes 6029312 | tf_op jit(solution)/shard_map/dot_general | solution.py:302
  144.2 4.0 %fusion.21 = f32[640,512]{1,0:T(8,128)} fusion(f32[1024,640]{1,0:T(8,128)S(1)} %get-tuple-element.78, f32[640]{0:T(1024)S(1)} %copy-done.48, f32[1024]{0:T(1024)S(1)} %fusion.105, f32[1024,512]{1,0:T(8,128)S(1)} %get-tuple-element.103, f32[1024,512]{1,0:T(8,128)S(1)} %fusion.24), kind=kOutput, calls=%fused_computation.51 | convolution fusion | flops 2019295232 | bytes 8133120 | tf_op jit(solution)/shard_map/dot_general | solution.py:302
  148.2 6.4 %convolution_add_fusion.x_ref = f32[1024,640]{1,0:T(8,128)S(1)} fusion(f32[1024,640]{1,0:T(8,128)} %fusion.139, f32[640,512]{1,0:T(8,128)} %param.28, f32[1024,512]{1,0:T(8,128)} %copy-done.36, f32[1024,512]{1,0:T(8,128)} %copy-done.13), kind=kOutput, calls=%fused_computation.50 | convolution fusion | flops 2018639872 | bytes 10747904 | tf_op jit(solution)/shard_map/dot_general | solution.py:302
  154.5 34.2 %shard_map.273 = f32[1024,640]{1,0:T(8,128)S(1)} custom-call(f32[1024,640]{1,0:T(8,128)S(1)} %convolution_add_fusion.x_ref), custom_call_target="tpu_custom_call" | custom-call | flops 1310720 | bytes 5242880 | tf_op jit(solution)/shard_map/pallas_call | solution.py:120
  191.4 1.9 multiply_reduce_fusion.2
  205.9 2.1 fusion.76
  208.0 2.6 fusion.80
  213.6 4.1 %fusion.3 = f32[768,640]{1,0:T(8,128)S(1)} fusion(f32[1024,640]{1,0:T(8,128)S(1)} %copy-done.8, f32[640]{0:T(1024)S(1)} %copy-done.50, f32[1024]{0:T(1024)S(1)} %fusion.101, f32[512,256]{0,1:T(8,128)S(1)} %slice.192, f32[512,256]{0,1:T(8,128)S(1)} %convolution_add_fusion.2, f32[1024,256]{0,1:T(8,128)S(1)} %fusion.43, f32[1024,256]{0,1:T(8,128)S(1)} %add_add_fusion.5), kind=kOutput, calls=%fused_computation.27 | convolution fusion | flops 3025928192 | bytes 7739904 | tf_op jit(solution)/shard_map/dot_general | solution.py:302
  219.8 10.2 %fusion.41 = f32[1024,640]{1,0:T(8,128)S(1)} fusion(f32[640,768]{1,0:T(8,128)} %copy-done.31, f32[512,256]{0,1:T(8,128)S(1)} %copy-done.47, f32[512,256]{0,1:T(8,128)} %copy-done.56, f32[1024,256]{0,1:T(8,128)} %copy-done.42, f32[1024,256]{0,1:T(8,128)} %copy-done.41), kind=kOutput, calls=%fused_computation.76 | convolution fusion | flops 3024617472 | bytes 7733248 | tf_op jit(solution)/shard_map/dot_general | solution.py:302
  230.3 48.3 %shard_map.274 = f32[1536,640]{1,0:T(8,128)S(1)} custom-call(f32[1536,640]{1,0:T(8,128)S(1)} %pad_maximum_fusion.x_ref), custom_call_target="tpu_custom_call" | custom-call | flops 1966080 | bytes 7864320 | tf_op jit(solution)/shard_map/pallas_call | solution.py:120
  278.7 1.9 copy-done.4
  282.8 4.8 %fusion.55 = f32[256,640]{1,0:T(8,128)} fusion(f32[512,256]{1,0:T(8,128)} %copy-done.24, f32[512,256]{1,0:T(8,128)S(1)} %copy-done.23, f32[1024,640]{1,0:T(8,128)S(1)} %copy-done.3, f32[1024,640]{1,0:T(8,128)} %copy-done.12, f32[1024]{0:T(1024)S(1)} %multiply_multiply_fusion.13, f32[640]{0:T(1024)S(1)} %copy-done.49, f32[1024]{0:T(1024)S(1)} %fusion.104), kind=kOutput, calls=%fused_computation.109 | convolution fusion | flops 1010171904 | bytes 6957568 | tf_op jit(solution)/shard_map/dot_general | solution.py:302
  287.6 4.1 %concatenate.43 = f32[648,640]{1,0:T(8,128)S(1)} concatenate(f32[256,640]{1,0:T(8,128)} %slice.196, f32[256,640]{1,0:T(8,128)} %fusion.55, f32[128,640]{1,0:T(8,128)S(1)} %constant_dynamic-slice_fusion, f32[1,640]{1,0:T(1,128)S(1)} %stack.5, f32[1,640]{1,0:T(1,128)S(1)} %reshape.305, f32[1,640]{1,0:T(1,128)S(1)} %reshape.306, f32[1,640]{1,0:T(1,128)S(1)} %reshape.307, ...), dimensions={0} | concatenate | bytes 3317760 | tf_op jit(solution)/shard_map/concatenate | solution.py:432
  291.8 64.9 %shard_map.275 = f32[704,640]{1,0:T(8,128)S(1)} custom-call(f32[704,640]{1,0:T(8,128)S(1)} %pad.32.x_ref), custom_call_target="tpu_custom_call" | custom-call | flops 901120 | bytes 3604480 | tf_op jit(solution)/shard_map/pallas_call | solution.py:275
  358.8 11.4 %shard_map.276 = f32[4,136,640]{2,1,0:T(8,128)S(1)} custom-call(f32[136,640]{1,0:T(8,128)S(1)} %slice.167.x_ref), custom_call_target="tpu_custom_call" | custom-call | bytes 1740800 | tf_op jit(solution)/shard_map/pallas_call | solution.py:178
  371.3 2.2 copy.57
  373.4 2.2 copy.56
  376.8 5.4 %fusion.2 = f32[1024,640]{1,0:T(8,128)} fusion(f32[1024,640]{1,0:T(8,128)} %copy-done.12, f32[1024,640]{1,0:T(8,128)} %param.16, f32[1536,640]{1,0:T(8,128)} %copy-done.4, f32[1024]{0:T(1024)S(1)} %multiply_multiply_fusion.10, f32[640]{0:T(1024)S(1)} %copy-done.50, f32[1024]{0:T(1024)S(1)} %fusion.101), kind=kLoop, calls=%fused_computation.11 | loop fusion | flops 3932160 | bytes 10496512 | tf_op jit(solution)/shard_map/add | solution.py:415
  382.3 2.6 copy.72
  (199 shorter events, 44.7 us)
Async XLA Ops:
  7.2 77.9 %copy-start = (f32[512,640]{1,0:T(8,128)S(1)}, f32[512,640]{1,0:T(8,128)}, u32[]{:S(2)}) copy-start(f32[512,640]{1,0:T(8,128)} %param.29) | copy-start | bytes 3932164
  7.2 4.6 %copy-start.43 = (f32[640,256]{1,0:T(8,128)S(1)}, f32[640,256]{1,0:T(8,128)}, u32[]{:S(2)}) copy-start(f32[640,256]{1,0:T(8,128)} %param.19) | copy-start | bytes 1966084
  7.2 4.7 %copy-start.44 = (f32[640,256]{1,0:T(8,128)S(1)}, f32[640,256]{1,0:T(8,128)}, u32[]{:S(2)}) copy-start(f32[640,256]{1,0:T(8,128)} %param.20) | copy-start | bytes 1966084
  7.2 375.0 %all-reduce.11.cloned.1.call-start = ((), (), s32[]{:S(2)}) async-start(), calls=%async_computation | async-start | bytes 7864320 | tf_op jit(solution)/shard_map/psum | solution.py:384
  11.8 6.0 %copy-start.52 = (s32[1024]{0:T(1024)}, s32[1024]{0:T(1024)S(1)}, u32[]{:S(2)}) copy-start(s32[1024]{0:T(1024)S(1)} %iota.39) | copy-start | bytes 12292
  13.5 4.4 %copy-start.31 = (f32[640,768]{1,0:T(8,128)}, f32[640,768]{1,0:T(8,128)S(1)}, u32[]{:S(2)}) copy-start(f32[640,768]{1,0:T(8,128)S(1)} %constant_dynamic-update-slice_fusion) | copy-start | bytes 5898244
  13.5 4.6 %copy-start.53 = (f32[256]{0:T(256)S(1)}, f32[256]{0:T(256)}, u32[]{:S(2)}) copy-start(f32[256]{0:T(256)} %param.23) | copy-start | bytes 3076
  13.5 4.6 %copy-start.54 = (f32[256]{0:T(256)S(1)}, f32[256]{0:T(256)}, u32[]{:S(2)}) copy-start(f32[256]{0:T(256)} %param.22) | copy-start | bytes 3076
  17.8 9.6 %copy-start.10 = (f32[1024,768]{0,1:T(8,128)}, f32[1024,768]{0,1:T(8,128)S(1)}, u32[]{:S(2)}) copy-start(f32[1024,768]{0,1:T(8,128)S(1)} %fusion.5) | copy-start | bytes 9437188
  18.4 4.5 %slice-start.1 = ((s32[1024]{0:T(1024)}), s32[512]{0:T(512)S(1)}, s32[]{:S(2)}) async-start(s32[1024]{0:T(1024)} %copy-done.52), calls=%async_computation.2 | async-start | bytes 4096 | tf_op jit(solution)/shard_map/slice | solution.py:350
  20.5 4.6 %copy-start.26 = (f32[1024,1,128]{0,2,1:T(8,128)}, f32[1024,1,128]{0,2,1:T(8,128)S(1)}, u32[]{:S(2)}) copy-start(f32[1024,1,128]{0,2,1:T(8,128)S(1)} %get-tuple-element.90) | copy-start | bytes 1572868
  20.5 4.6 %copy-start.28 = (f32[1024,1,128]{0,2,1:T(8,128)}, f32[1024,1,128]{0,2,1:T(8,128)S(1)}, u32[]{:S(2)}) copy-start(f32[1024,1,128]{0,2,1:T(8,128)S(1)} %get-tuple-element.91) | copy-start | bytes 1572868
  25.1 3.6 copy-start.21
  28.7 36.5 %copy-start.24 = (f32[512,256]{1,0:T(8,128)}, f32[512,256]{1,0:T(8,128)S(1)}, u32[]{:S(2)}) copy-start(f32[512,256]{1,0:T(8,128)S(1)} %fusion.49) | copy-start | bytes 1572868
  66.8 77.4 %copy-start.5 = (f32[1024,640]{1,0:T(8,128)}, f32[1024,640]{1,0:T(8,128)S(1)}, u32[]{:S(2)}) copy-start(f32[1024,640]{1,0:T(8,128)S(1)} %get-tuple-element.78) | copy-start | bytes 7864324
  67.5 2.7 copy-start.18
  70.2 74.0 %copy-start.13 = (f32[1024,512]{1,0:T(8,128)}, f32[1024,512]{1,0:T(8,128)S(1)}, u32[]{:S(2)}) copy-start(f32[1024,512]{1,0:T(8,128)S(1)} %fusion.24) | copy-start | bytes 6291460
  135.8 8.3 %copy-start.36 = (f32[1024,512]{1,0:T(8,128)}, f32[1024,512]{1,0:T(8,128)S(1)}, u32[]{:S(2)}) copy-start(f32[1024,512]{1,0:T(8,128)S(1)} %get-tuple-element.103) | copy-start | bytes 6291460
  154.5 34.2 %copy-start.6 = (f32[1024,640]{1,0:T(8,128)S(1)}, f32[1024,640]{1,0:T(8,128)}, u32[]{:S(2)}) copy-start(f32[1024,640]{1,0:T(8,128)} %copy-done.5) | copy-start | bytes 7864324
  188.8 2.6 copy-start.15
  193.3 4.3 %copy-start.12 = (f32[1024,640]{1,0:T(8,128)}, f32[1024,640]{1,0:T(8,128)S(1)}, u32[]{:S(2)}) copy-start(f32[1024,640]{1,0:T(8,128)S(1)} %get-tuple-element.76) | copy-start | bytes 7864324
  193.4 2.8 copy-start.35
  198.4 13.3 %copy-start.56 = (f32[512,256]{0,1:T(8,128)}, f32[512,256]{0,1:T(8,128)S(1)}, u32[]{:S(2)}) copy-start(f32[512,256]{0,1:T(8,128)S(1)} %convolution_add_fusion.2) | copy-start | bytes 1572868
  198.5 13.3 %copy-start.46 = (f32[512,256]{0,1:T(8,128)}, f32[512,256]{0,1:T(8,128)S(1)}, u32[]{:S(2)}) copy-start(f32[512,256]{0,1:T(8,128)S(1)} %slice.192) | copy-start | bytes 1572868
  211.5 6.3 %copy-start.41 = (f32[1024,256]{0,1:T(8,128)}, f32[1024,256]{0,1:T(8,128)S(1)}, u32[]{:S(2)}) copy-start(f32[1024,256]{0,1:T(8,128)S(1)} %add_add_fusion.5) | copy-start | bytes 3145732
  213.6 4.1 %copy-start.42 = (f32[1024,256]{0,1:T(8,128)}, f32[1024,256]{0,1:T(8,128)S(1)}, u32[]{:S(2)}) copy-start(f32[1024,256]{0,1:T(8,128)S(1)} %fusion.43) | copy-start | bytes 3145732
  219.8 10.2 %copy-start.17 = (f32[512,640]{1,0:T(8,128)S(1)}, f32[512,640]{1,0:T(8,128)}, u32[]{:S(2)}) copy-start(f32[512,640]{1,0:T(8,128)} %slice.195) | copy-start | bytes 3932164
  230.3 50.2 %copy-start.9 = (f32[1024,640]{1,0:T(8,128)S(1)}, f32[1024,640]{1,0:T(8,128)}, u32[]{:S(2)}) copy-start(f32[1024,640]{1,0:T(8,128)} %param.16) | copy-start | bytes 7864324
  370.1 6.7 %copy-start.51 = (f32[1024]{0:T(1024)S(1)}, f32[1024]{0:T(1024)}, u32[]{:S(2)}) copy-start(f32[1024]{0:T(1024)} %get-tuple-element.54) | copy-start | bytes 12292
  382.3 2.6 copy-start.38
  382.3 3.7 copy-start.37
  382.3 4.7 %copy-start.1 = (f32[512,640]{1,0:T(8,128)S(1)}, f32[512,640]{1,0:T(8,128)}, u32[]{:S(2)}) copy-start(f32[512,640]{1,0:T(8,128)} %param.29) | copy-start | bytes 3932164
  (28 other events, 48.9 us)
Sparse Core Ops, SparseCore 0:
  154.7 154.4 all-reduce.10
